TPU v7x, 256 devices: a whole 4x4x8 slice. The times are simulated.
256 devices in a mesh: lon: 64 (over y_lo, z, x), lat: 4 (over y_hi, core).
Axes of the slice: x: 4, y: 4 (y_hi: 2, y_lo: 2; y = y_hi * 2 + y_lo), z: 8, core: 2. Of those that a mesh axis runs over, the one named last changes fastest.
Arguments:
- tokens: bfloat16 [2, 24, 3072, 384], P(None, 'lat', 'lon'), may hold values from -6 to 6
- cotangent: bfloat16 [2, 24, 3072, 384], P(None, 'lat', 'lon'), may hold values from -40 to 40
- mask_ids: int32 [2, 24], P(None, 'lat'), may hold values from 0 to 1
- band_type: int32 [4], replicated, may hold values from 0 to 3, each once
- bias_table: bfloat16 [4, 12, 3312], replicated, may hold values from -4 to 4
- w_qkv: bfloat16 [384, 1152], replicated, may hold values from -0.3125 to 0.3125
- w_proj: bfloat16 [384, 384], replicated, may hold values from -0.3125 to 0.3125
- ln_gain: float32 [384], replicated, may hold values from 0.5 to 1.5
- ln_shift: float32 [384], replicated, may hold values from -1.5 to 1.5
Outputs:
- grad_tokens: bfloat16 [2, 24, 3072, 384], P(None, 'lat', 'lon')
- grad_qkv: bfloat16 [384, 1152], replicated
- grad_proj: bfloat16 [384, 384], replicated
- grad_gain: float32 [384], replicated
- grad_shift: float32 [384], replicated
- grad_table: bfloat16 [4, 12, 3312], replicated
All inputs are finite; a program needn't handle non-finite values.
Results may differ from a plain program's by a relative error of at most 0.0089.
Values may be sent and summed in bfloat16 or wider, within the bound.
A program may use at most 128 MiB of HBM per device.

v0:
```python
import jax
import jax.numpy as jnp
from jax import lax
from jax.sharding import PartitionSpec as P

WPL = 2
WLAT = 6
WLON = 12


EPSILON = 1e-05


def partner(block, axis, stride):
    count = lax.axis_size(axis)
    route = []
    for low in range(count):
        high = low | 1 << stride
        if high != low and high < count:
            route += [(low, high), (high, low)]
    return lax.ppermute(block, axis, route)


def shifted_2(value, axis, steps):
    count = lax.axis_size(axis)
    pairs = [(source, (source + steps) % count) for source in range(count)]
    return lax.ppermute(value, axis, pairs)


def offset_table():
    spread = 2 * WLON - 1
    first = jnp.arange(WLON, dtype=jnp.int32)
    pairs = (first[:, None] - first[None, :] + WLON - 1).reshape(-1)
    return (jnp.arange(spread, dtype=jnp.int32)[:, None] == pairs[None, :]).astype(jnp.float32)


def expand_bias(bias_rows):
    outer = bias_rows.shape[:3]
    grouped = bias_rows.reshape(outer + (WPL * WPL * WLAT * WLAT, 2 * WLON - 1))
    spread_out = jnp.einsum(
        "pahsd,de->pahse", grouped, offset_table(), precision=lax.Precision.HIGHEST
    )
    spread_out = spread_out.reshape(outer + (WPL, WPL, WLAT, WLAT, WLON, WLON))
    spread_out = spread_out.transpose(0, 1, 2, 3, 5, 7, 4, 6, 8)
    window = WPL * WLAT * WLON
    return spread_out.reshape(outer + (window, window))


def fold_bias(d_bias):
    outer = d_bias.shape[:3]
    split_up = d_bias.reshape(outer + (WPL, WLAT, WLON, WPL, WLAT, WLON)).transpose(
        0, 1, 2, 3, 6, 4, 7, 5, 8
    )
    split_up = split_up.reshape(outer + (WPL * WPL * WLAT * WLAT, WLON * WLON))
    folded = jnp.einsum(
        "pahse,de->pahsd", split_up, offset_table(), precision=lax.Precision.HIGHEST
    )
    return folded.reshape(outer + (-1,))


def to_windows(grid):
    planes, lat_rows, lon_cols, channels = grid.shape
    split_up = grid.reshape(
        planes // WPL, WPL, lat_rows // WLAT, WLAT, lon_cols // WLON, WLON, channels
    )
    split_up = split_up.transpose(0, 2, 4, 1, 3, 5, 6)
    return split_up.reshape(
        planes // WPL, lat_rows // WLAT, lon_cols // WLON, WPL * WLAT * WLON, channels
    )


def from_windows(windows, planes, lat_rows, lon_cols):
    channels = windows.shape[-1]
    split_up = windows.reshape(
        planes // WPL, lat_rows // WLAT, lon_cols // WLON, WPL, WLAT, WLON, channels
    )
    return split_up.transpose(0, 3, 1, 4, 2, 5, 6).reshape(planes, lat_rows, lon_cols, channels)


def batched(form, left, right):
    return jnp.einsum(form, left, right, preferred_element_type=jnp.float32)


def block_backward(shifted, shifted_cot, region_ids, bias_rows, w_qkv, w_proj, ln_gain, ln_shift):
    planes, lat_rows, lon_cols, channels = shifted.shape
    head_count = bias_rows.shape[2]
    head_dim = channels // head_count
    window = WPL * WLAT * WLON
    score_scale = head_dim ** (-0.5)
    flat_in = shifted.reshape(-1, channels).astype(jnp.float32)
    average = jnp.mean(flat_in, axis=1, keepdims=True)
    centred = flat_in - average
    variance = jnp.mean(centred * centred, axis=1, keepdims=True)
    inv_std = lax.rsqrt(variance + EPSILON)
    normed = centred * inv_std
    ln_out = (normed * ln_gain + ln_shift).astype(jnp.bfloat16)
    qkv = jnp.dot(ln_out, w_qkv, preferred_element_type=jnp.float32).astype(jnp.bfloat16)
    qkv_win = to_windows(qkv.reshape(planes, lat_rows, lon_cols, 3 * channels))
    lead = qkv_win.shape[:3]
    queries = qkv_win[..., :channels].reshape(lead + (window, head_count, head_dim))
    keys = qkv_win[..., channels : 2 * channels].reshape(lead + (window, head_count, head_dim))
    values = qkv_win[..., 2 * channels :].reshape(lead + (window, head_count, head_dim))
    bias = expand_bias(bias_rows)
    ids_grid = region_ids.reshape(planes // WPL, WPL, lat_rows // WLAT, WLAT).transpose(0, 2, 1, 3)
    ids_win = jnp.broadcast_to(ids_grid[..., None], ids_grid.shape + (WLON,)).reshape(
        planes // WPL, lat_rows // WLAT, window
    )
    allowed = (ids_win[:, :, :, None] == ids_win[:, :, None, :])[:, :, None, None]
    scores = batched("pawqhd,pawkhd->pawhqk", queries, keys) * score_scale + bias[:, :, None]
    raised = jnp.where(allowed, jnp.exp(scores), 0.0)
    probs = raised / jnp.sum(raised, axis=-1, keepdims=True)
    probs_b = probs.astype(jnp.bfloat16)
    attended = batched("pawhqk,pawkhd->pawqhd", probs_b, values).astype(jnp.bfloat16)
    attended = attended.reshape(-1, channels)
    cot_win = to_windows(shifted_cot)
    cot_flat = cot_win.reshape(-1, channels)
    grad_proj = lax.dot_general(
        attended, cot_flat, (((0,), (0,)), ((), ())), preferred_element_type=jnp.float32
    )
    d_attended = lax.dot_general(
        cot_flat, w_proj, (((1,), (1,)), ((), ())), preferred_element_type=jnp.float32
    )
    d_attended = d_attended.astype(jnp.bfloat16).reshape(lead + (window, head_count, head_dim))
    d_probs = batched("pawqhd,pawkhd->pawhqk", d_attended, values)
    d_values = batched("pawhqk,pawqhd->pawkhd", probs_b, d_attended)
    d_scores = probs * (d_probs - jnp.sum(probs * d_probs, axis=-1, keepdims=True))
    d_scores_b = d_scores.astype(jnp.bfloat16)
    d_queries = batched("pawhqk,pawkhd->pawqhd", d_scores_b, keys) * score_scale
    d_keys = batched("pawhqk,pawqhd->pawkhd", d_scores_b, queries) * score_scale
    d_qkv_win = jnp.concatenate(
        [
            d_queries.reshape(lead + (window, channels)),
            d_keys.reshape(lead + (window, channels)),
            d_values.reshape(lead + (window, channels)),
        ],
        axis=-1,
    ).astype(jnp.bfloat16)
    d_qkv = from_windows(d_qkv_win, planes, lat_rows, lon_cols).reshape(-1, 3 * channels)
    grad_qkv = lax.dot_general(
        ln_out, d_qkv, (((0,), (0,)), ((), ())), preferred_element_type=jnp.float32
    )
    d_ln = lax.dot_general(
        d_qkv, w_qkv, (((1,), (1,)), ((), ())), preferred_element_type=jnp.float32
    )
    grad_gain = jnp.sum(d_ln * normed, axis=0)
    grad_shift = jnp.sum(d_ln, axis=0)
    scaled = d_ln * ln_gain
    d_flat = inv_std * (
        scaled
        - jnp.mean(scaled, axis=1, keepdims=True)
        - normed * jnp.mean(scaled * normed, axis=1, keepdims=True)
    )
    d_shifted = d_flat.astype(jnp.bfloat16).reshape(planes, lat_rows, lon_cols, channels)
    d_rows = fold_bias(jnp.sum(d_scores, axis=2))
    return (d_shifted, grad_qkv, grad_proj, grad_gain, grad_shift, d_rows)


def local(tokens, cotangent, mask_ids, band_type, bias_table, w_qkv, w_proj, ln_gain, ln_shift):
    half_lon = WLON // 2
    half_lat = WLAT // 2
    stacked = jnp.roll(jnp.stack([tokens, cotangent]), -(WPL // 2), axis=1)
    incoming = partner(stacked[:, :, :, :half_lon], "lon", 0)
    stacked = jnp.concatenate([stacked[:, :, :, half_lon:], incoming], axis=3)
    incoming = shifted_2(stacked[:, :, :half_lat], "lat", -1)
    stacked = jnp.concatenate([stacked[:, :, half_lat:], incoming], axis=2)
    shifted = stacked[0]
    shifted_cot = stacked[1]
    level_bands = tokens.shape[0] // WPL
    own_bands = tokens.shape[1] // WLAT
    band_start = lax.axis_index("lat") * own_bands
    local_bands = lax.dynamic_slice_in_dim(band_type, band_start, own_bands)
    type_ids = (
        local_bands[None, :] * level_bands + jnp.arange(level_bands, dtype=jnp.int32)[:, None]
    )
    bias_rows = bias_table[type_ids].astype(jnp.float32)
    d_shifted, g_qkv, g_proj, g_gain, g_shift, d_rows = block_backward(
        shifted, shifted_cot, mask_ids, bias_rows, w_qkv, w_proj, ln_gain, ln_shift
    )
    type_total = bias_table.shape[0]
    head_count = bias_table.shape[1]
    positions = bias_table.shape[2]
    selector = (
        jnp.arange(type_total, dtype=jnp.int32)[:, None] == type_ids.reshape(-1)[None, :]
    ).astype(jnp.float32)
    table_part = jnp.dot(
        selector, d_rows.reshape(-1, head_count * positions), precision=lax.Precision.HIGHEST
    )
    table_part = table_part.reshape(type_total, head_count, positions)
    g_qkv, g_proj, g_gain, g_shift, g_table = lax.psum(
        (g_qkv, g_proj, g_gain, g_shift, table_part), ("lon", "lat")
    )
    incoming = shifted_2(d_shifted[:, -half_lat:], "lat", 1)
    d_shifted = jnp.concatenate([incoming, d_shifted[:, :-half_lat]], axis=1)
    incoming = partner(d_shifted[:, :, -half_lon:], "lon", 0)
    d_shifted = jnp.concatenate([incoming, d_shifted[:, :, :-half_lon]], axis=2)
    d_shifted = jnp.roll(d_shifted, WPL // 2, axis=0)
    grad_tokens = (cotangent.astype(jnp.float32) + d_shifted.astype(jnp.float32)).astype(
        jnp.bfloat16
    )
    return (
        grad_tokens,
        g_qkv.astype(jnp.bfloat16),
        g_proj.astype(jnp.bfloat16),
        g_gain,
        g_shift,
        g_table.astype(jnp.bfloat16),
    )


def solution(mesh):
    placed = (
        P(None, "lat", "lon", None),
        P(None, "lat", "lon", None),
        P(None, "lat"),
        P(),
        P(),
        P(),
        P(),
        P(),
        P(),
    )
    return jax.shard_map(
        local,
        mesh=mesh,
        in_specs=placed,
        out_specs=(P(None, "lat", "lon", None), P(), P(), P(), P(), P()),
        check_vma=False,
    )
```

profile of v0, /device:TPU:1, one launch (start us, length us, event | category | flops | bytes accessed | tf_op | source)
XLA Modules:
  0.0 327.7 jit_solution(13687017706977451809)
XLA Ops:
  2.7 2.1 collective-permute-start
  12.5 7.0 %convolution_bitcast_fusion = f32[1,1,12,2,6,12,2,6,12]{8,2,5,7,4,6,3,1,0:T(8,128)} fusion(bf16[12,2,2,6,6,23,1]{5,4,3,2,1,0,6:T(8,128)(2,1)S(1)} %bitcast.92, pred[12,12,23,1,1,1,1]{2,1,0,3,4,5,6:T(8,128)(4,1)S(1)} %reshape.411), kind=kOutput, calls=%fused_computation.3 | convolution fusion | flops 11446272 | bytes 1078128 | tf_op jit(solution)/shard_map/pahsd,de->pahse/dot_general | solution.py:40
  19.5 21.1 %copy.77 = f32[1,1,12,2,6,12,2,6,12]{5,4,3,8,7,6,2,1,0:T(8,128)} copy(f32[1,1,12,2,6,12,2,6,12]{8,2,5,7,4,6,3,1,0:T(8,128)} %convolution_bitcast_fusion) | data formatting | bytes 1990656 | tf_op jit(solution)/shard_map/add | solution.py:109
  40.6 9.3 %reshape.414 = f32[12,144,144]{1,2,0:T(8,128)S(1)} reshape(f32[1,1,12,2,6,12,2,6,12]{5,4,3,8,7,6,2,1,0:T(8,128)} %copy.77) | data formatting | bytes 1990656 | tf_op jit(solution)/shard_map/add | solution.py:109
  58.2 2.2 convolution_convert_fusion.1
  62.3 3.1 reshape.378
  67.2 2.6 convolution_convert_fusion
  69.8 3.2 reshape_reshape.10
  76.4 2.2 copy.46
  78.6 2.2 copy.45
  80.7 2.2 copy.53
  82.9 3.6 %fusion.1 = (f32[4,12,144]{2,1,0:T(8,128)S(1)}, f32[4,12,144,144]{2,3,1,0:T(8,128)S(1)}) fusion(f32[12,144,144]{1,2,0:T(8,128)S(1)} %reshape.414, pred[144,144]{0,1:T(8,128)(4,1)} %broadcast_compare_fusion, bf16[4,144,12,32]{1,3,2,0:T(8,128)(2,1)} %bitcast.99, bf16[4,144,12,32]{1,3,2,0:T(8,128)(2,1)} %bitcast.94), kind=kOutput, calls=%fused_computation.5 | convolution fusion | flops 67675392 | bytes 5909760 | tf_op jit(solution)/shard_map/pawqhd,pawkhd->pawhqk/dot_general | solution.py:81
  86.6 3.0 fusion.17
  89.6 2.7 multiply_reduce_fusion
  92.3 4.4 %fusion.2 = (f32[12,144,144]{1,2,0:T(8,128)S(1)}, bf16[4,12,144,144]{2,3,1,0:T(8,128)(2,1)S(1)}) fusion(f32[4,12,144,144]{2,3,1,0:T(8,128)S(1)} %get-tuple-element.44, f32[4,12,144]{2,1,0:T(8,128)S(1)} %get-tuple-element.43, f32[4,12,144]{2,1,0:T(8,128)S(1)} %get-tuple-element.41, f32[12,144,144]{1,2,0:T(8,128)} %copy-done.1, ...), kind=kLoop, calls=%fused_computation.7 | loop fusion | flops 7713792 | bytes 12019968 | tf_op jit(solution)/shard_map/reduce_sum | solution.py:154
  96.8 2.1 fusion.21
  101.4 3.0 fusion.14
  104.4 5.2 %copy.61 = bf16[1,1,4,144,12,32]{5,4,2,3,1,0:T(8,128)(2,1)} copy(bf16[1,1,4,144,12,32]{3,5,4,2,1,0:T(8,128)(2,1)} %fusion.17) | data formatting | bytes 884736 | tf_op jit(solution)/shard_map/pawhqk,pawqhd->pawkhd/transpose | solution.py:81
  109.6 4.1 %concatenate.44 = bf16[1,1,4,2,6,12,384]{6,2,5,4,3,1,0:T(4,128)(2,1)} reshape(bf16[1,1,4,144,12,32]{5,4,2,3,1,0:T(8,128)(2,1)} %copy.61) | data formatting | bytes 884736 | tf_op jit(solution)/shard_map/concatenate | solution.py:130
  113.7 5.2 %copy.58 = bf16[1,1,4,144,12,32]{5,4,2,3,1,0:T(8,128)(2,1)} copy(bf16[1,1,4,144,12,32]{3,5,4,2,1,0:T(8,128)(2,1)} %fusion.21) | data formatting | bytes 884736 | tf_op jit(solution)/shard_map/mul | solution.py:129
  118.9 4.1 %concatenate.43 = bf16[1,1,4,2,6,12,384]{6,2,5,4,3,1,0:T(4,128)(2,1)} reshape(bf16[1,1,4,144,12,32]{5,4,2,3,1,0:T(8,128)(2,1)} %copy.58) | data formatting | bytes 884736 | tf_op jit(solution)/shard_map/concatenate | solution.py:130
  123.1 5.4 %copy.56 = bf16[1,1,4,144,12,32]{5,4,2,3,1,0:T(8,128)(2,1)} copy(bf16[1,1,4,144,12,32]{3,5,4,2,1,0:T(8,128)(2,1)} %fusion.20) | data formatting | bytes 884736 | tf_op jit(solution)/shard_map/mul | solution.py:128
  128.4 4.1 %concatenate.42 = bf16[1,1,4,2,6,12,384]{6,2,5,4,3,1,0:T(4,128)(2,1)} reshape(bf16[1,1,4,144,12,32]{5,4,2,3,1,0:T(8,128)(2,1)} %copy.56) | data formatting | bytes 884736 | tf_op jit(solution)/shard_map/concatenate | solution.py:130
  136.0 3.4 %reshape_reshape.12 = bf16[576,1152]{1,0:T(8,128)(2,1)} reshape(bf16[1,2,1,6,4,12,1152]{6,5,4,3,1,2,0:T(8,128)(2,1)} %copy.62) | data formatting | bytes 2654208 | tf_op jit(solution)/shard_map/reshape;reshape | solution.py:138
  139.4 3.4 %fusion.42 = (f32[384]{0:T(512)S(1)}, f32[384]{0:T(512)}, f32[576]{0:T(1024)S(1)}, f32[576]{0:T(1024)S(1)}, f32[576,384]{1,0:T(8,128)S(1)}) fusion(f32[576]{0:T(1024)S(1)} %copy-done.16, f32[576]{0:T(1024)S(1)} %copy-done.15, bf16[1,2,6,48,384]{4,3,2,1,0:T(8,128)(2,1)S(1)} %get-tuple-element.29, f32[576,384]{1,0:T(8,128)} %copy-done.5, ...), kind=kOutput, calls=%fused_computation.73 | convolution fusion | flops 511817856 | bytes 4437504 | tf_op jit(solution)/shard_map/dot_general | solution.py:142
  144.1 2.5 collective-permute-start.2
  146.6 2.2 fusion.47
  150.3 2.9 reshape.381
  155.2 10.1 %reshape.383 = f32[1,1,12,2,6,12,2,6,12]{8,7,6,5,4,3,2,1,0:T(8,128)} reshape(f32[12,144,144]{2,1,0:T(8,128)} %copy.65) | data formatting | bytes 1990656 | tf_op jit(solution)/shard_map/reshape | solution.py:51
  165.3 14.1 %copy.66 = f32[1,1,12,2,2,6,6,12,12]{8,7,6,5,4,3,2,1,0:T(8,128)} copy(f32[1,1,12,2,2,6,6,12,12]{8,6,4,7,5,3,2,1,0:T(8,128)} %bitcast.87) | data formatting | bytes 1990656 | tf_op jit(solution)/shard_map/transpose | solution.py:51
  179.4 9.3 %reshape.384 = f32[12,144,144]{2,1,0:T(8,128)S(1)} reshape(f32[1,1,12,2,2,6,6,12,12]{8,7,6,5,4,3,2,1,0:T(8,128)} %copy.66) | data formatting | bytes 1990656 | tf_op jit(solution)/shard_map/reshape.54
  195.0 130.4 %all-reduce.2 = (bf16[384,1152]{1,0:T(8,128)(2,1)}, bf16[384,384]{1,0:T(8,128)(2,1)}, f32[384]{0:T(512)}, f32[384]{0:T(512)}, bf16[4,12,3312]{2,0,1:T(4,128)(2,1)}) all-reduce(f32[384,1152]{1,0:T(8,128)} %fusion.47, f32[384,384]{1,0:T(8,128)S(1)} %fusion.48, f32[384]{0:T(512)S(1)} %copy-done.22, ...), channel_id=1, replica_groups=mesh['lon'=64,'lat'=4] {'lon','lat'}, use_global_device_ids=true, to_apply=%region_6.7 | all-reduce | flops 749568 | bytes 4498944 | tf_op jit(solution)/shard_map/psum | solution.py:189
  (105 shorter events, 41.9 us)
Async XLA Ops:
  0.6 66.6 %copy-start = (bf16[384,1152]{1,0:T(8,128)(2,1)S(1)}, bf16[384,1152]{1,0:T(8,128)(2,1)}, u32[]{:S(2)}) copy-start(bf16[384,1152]{1,0:T(8,128)(2,1)} %param.14) | copy-start | bytes 2654212
  0.6 5.8 %copy-start.25 = (s32[4]{0:T(128)S(1)}, s32[4]{0:T(128)}, u32[]{:S(2)}) copy-start(s32[4]{0:T(128)} %param.12) | copy-start | bytes 52
  0.7 8.3 %copy-start.14 = (bf16[4,12,3312]{2,0,1:T(4,128)(2,1)S(1)}, bf16[4,12,3312]{2,0,1:T(4,128)(2,1)}, u32[]{:S(2)}) copy-start(bf16[4,12,3312]{2,0,1:T(4,128)(2,1)} %param.13) | copy-start | bytes 953860
  2.7 7.7 %collective-permute-start = (bf16[2,2,6,6,384]{4,3,2,1,0:T(8,128)(2,1)S(1)}, bf16[2,2,6,6,384]{4,3,2,1,0:T(8,128)(2,1)S(1)}, u32[]{:S(2)}, u32[]{:S(2)}) collective-permute-start(bf16[2,2,6,6,384]{4,3,2,1,0:T(8,128)(2,1)S(1)} %pad_maximum_fusion.4), channel_id=1, source_target_pairs={{0,4},{4,0},{8,12},{12,8},{16,20},{20,16},{24,28},{28,24},{32,36},... | collective-permute-start | bytes 331784 | tf_op jit(solution)/shard_map/ppermute | solution.py:21
  4.9 4.1 %copy-start.19 = (s32[144]{0:T(256)}, s32[144]{0:T(256)S(1)}, u32[]{:S(2)}) copy-start(s32[144]{0:T(256)S(1)} %sub.86) | copy-start | bytes 1732
  11.2 40.7 %collective-permute-start.1 = (bf16[2,2,3,48,384]{4,3,2,1,0:T(8,128)(2,1)}, bf16[2,2,3,48,384]{4,3,2,1,0:T(8,128)(2,1)}, u32[]{:S(2)}, u32[]{:S(2)}) collective-permute-start(bf16[2,2,3,48,384]{4,3,2,1,0:T(8,128)(2,1)} %get-tuple-element.36), channel_id=1, source_target_pairs={{0,3},{1,0},{2,1},{3,2},{4,7},{5,4},{6,5},{7,6},{8,11},{9,8},{10,9... | collective-permute-start | bytes 1327112 | tf_op jit(solution)/shard_map/ppermute | solution.py:27
  40.6 9.3 %copy-start.23 = (s32[2,6]{1,0:T(2,128)S(1)}, s32[2,6]{1,0:T(2,128)}, u32[]{:S(2)}) copy-start(s32[2,6]{1,0:T(2,128)} %param.11) | copy-start | bytes 148
  49.9 39.7 %copy-start.1 = (f32[12,144,144]{1,2,0:T(8,128)}, f32[12,144,144]{1,2,0:T(8,128)S(1)}, u32[]{:S(2)}) copy-start(f32[12,144,144]{1,2,0:T(8,128)S(1)} %reshape.414) | copy-start | bytes 2985988
  66.3 0.9 copy-start.5
  82.9 3.6 %copy-start.10 = (bf16[4,144,12,32]{1,0,3,2:T(4,128)(2,1)S(1)}, bf16[4,144,12,32]{1,0,3,2:T(4,128)(2,1)}, u32[]{:S(2)}) copy-start(bf16[4,144,12,32]{1,0,3,2:T(4,128)(2,1)} %reshape.378) | copy-start | bytes 1327108
  82.9 3.7 %copy-start.13 = (pred[144,144]{0,1:T(8,128)(4,1)S(1)}, pred[144,144]{0,1:T(8,128)(4,1)}, u32[]{:S(2)}) copy-start(pred[144,144]{0,1:T(8,128)(4,1)} %broadcast_compare_fusion) | copy-start | bytes 62212
  86.6 3.1 copy-start.11
  92.3 4.5 %copy-start.6 = (bf16[1,1,4,144,384]{3,4,2,1,0:T(8,128)(2,1)S(1)}, bf16[1,1,4,144,384]{3,4,2,1,0:T(8,128)(2,1)}, u32[]{:S(2)}) copy-start(bf16[1,1,4,144,384]{3,4,2,1,0:T(8,128)(2,1)} %copy.46) | copy-start | bytes 1327108
  96.8 2.1 copy-start.4
  98.9 1.5 copy-start.17
  98.9 1.5 copy-start.21
  98.9 2.5 copy-start.2
  134.5 4.9 %copy-start.15 = (f32[576]{0:T(1024)S(1)}, f32[576]{0:T(1024)}, u32[]{:S(2)}) copy-start(f32[576]{0:T(1024)} %div.25) | copy-start | bytes 6916
  134.5 4.9 %copy-start.16 = (f32[576]{0:T(1024)S(1)}, f32[576]{0:T(1024)}, u32[]{:S(2)}) copy-start(f32[576]{0:T(1024)} %rsqrt.13) | copy-start | bytes 6916
  134.5 4.9 %copy-start.18 = (f32[384]{0:T(512)S(1)}, f32[384]{0:T(512)}, u32[]{:S(2)}) copy-start(f32[384]{0:T(512)} %param.16) | copy-start | bytes 4612
  139.4 7.2 %copy-start.8 = (bf16[576,1152]{1,0:T(8,128)(2,1)S(1)}, bf16[576,1152]{1,0:T(8,128)(2,1)}, u32[]{:S(2)}) copy-start(bf16[576,1152]{1,0:T(8,128)(2,1)} %reshape_reshape.12) | copy-start | bytes 3981316
  139.4 7.2 %copy-start.12 = (bf16[1,2,6,48,384]{4,3,2,1,0:T(8,128)(2,1)S(1)}, bf16[1,2,6,48,384]{4,3,2,1,0:T(8,128)(2,1)}, u32[]{:S(2)}) copy-start(bf16[1,2,6,48,384]{4,3,2,1,0:T(8,128)(2,1)} %add_convert_fusion) | copy-start | bytes 1327108
  142.9 6.0 %copy-start.9 = (bf16[1,1,4,144,12,32]{3,5,4,2,1,0:T(8,128)(2,1)S(1)}, bf16[1,1,4,144,12,32]{3,5,4,2,1,0:T(8,128)(2,1)}, u32[]{:S(2)}) copy-start(bf16[1,1,4,144,12,32]{3,5,4,2,1,0:T(8,128)(2,1)} %fusion.14) | copy-start | bytes 1327108
  144.1 49.8 %collective-permute-start.2 = (bf16[2,3,48,384]{3,2,1,0:T(8,128)(2,1)}, bf16[2,3,48,384]{3,2,1,0:T(8,128)(2,1)}, u32[]{:S(2)}, u32[]{:S(2)}) collective-permute-start(bf16[2,3,48,384]{3,2,1,0:T(8,128)(2,1)} %get-tuple-element.39), channel_id=1, source_target_pairs={{0,1},{1,2},{2,3},{3,0},{4,5},{5,6},{6,7},{7,4},{8,9},{9,10},{10,1... | collective-permute-start | bytes 663560 | tf_op jit(solution)/shard_map/ppermute | solution.py:27
  179.4 9.3 %copy-start.20 = (s32[144]{0:T(256)S(1)}, s32[144]{0:T(256)}, u32[]{:S(2)}) copy-start(s32[144]{0:T(256)} %copy-done.19) | copy-start | bytes 1732
  188.7 3.5 %copy-start.24 = (f32[4]{0:T(128)S(1)}, f32[4]{0:T(128)}, u32[]{:S(2)}) copy-start(f32[4]{0:T(128)} %fusion.39) | copy-start | bytes 52
  188.7 5.2 %copy-start.7 = (bf16[2,3,48,384]{3,2,1,0:T(8,128)(2,1)S(1)}, bf16[2,3,48,384]{3,2,1,0:T(8,128)(2,1)}, u32[]{:S(2)}) copy-start(bf16[2,3,48,384]{3,2,1,0:T(8,128)(2,1)} %get-tuple-element.40) | copy-start | bytes 663556
  188.7 6.3 %copy-start.22 = (f32[384]{0:T(512)S(1)}, f32[384]{0:T(512)}, u32[]{:S(2)}) copy-start(f32[384]{0:T(512)} %get-tuple-element.20) | copy-start | bytes 4612
  192.3 134.2 %copy-start.3 = (bf16[2,6,48,384]{3,2,1,0:T(8,128)(2,1)S(1)}, bf16[2,6,48,384]{3,2,1,0:T(8,128)(2,1)}, u32[]{:S(2)}) copy-start(bf16[2,6,48,384]{3,2,1,0:T(8,128)(2,1)} %param.10) | copy-start | bytes 1327108
  194.7 130.7 %collective-permute-start.3 = (bf16[2,6,6,384]{3,2,1,0:T(8,128)(2,1)S(1)}, bf16[2,6,6,384]{3,2,1,0:T(8,128)(2,1)S(1)}, u32[]{:S(2)}, u32[]{:S(2)}) collective-permute-start(bf16[2,6,6,384]{3,2,1,0:T(8,128)(2,1)S(1)} %pad_maximum_fusion.5), channel_id=1, source_target_pairs={{0,4},{4,0},{8,12},{12,8},{16,20},{20,16},{24,28},{28,24},{32,36},... | collective-permute-start | bytes 165896 | tf_op jit(solution)/shard_map/ppermute | solution.py:21
where the time goes:
time: 334 us; the launch traced here: 328 us
  local copies, waits for them, and re-layouts  131 us (39%)
  blocking collectives  130 us (39%)
  matrix products  36.8 us (11%)
  other arithmetic  20 us (6%)
  starting transfers between devices  6.23 us (2%)
    psum x1, blocking collectives, local(): lax.psum((g_qkv, g_proj, g_gain, g_shift, table_part), ('lon', 'lat'))  130 us
    add x2, local copies, waits for them, and re-layouts, block_backward(): batched('pawqhd,pawkhd->pawhqk', queries, keys) * score_scale  30.4 us
    dot_general x6, matrix products, batched(): return jnp.einsum(form, left, right, preferred_element_type=jnp.float32)  15.9 us
    transpose x1, local copies, waits for them, and re-layouts, fold_bias(): d_bias.reshape(outer + (WPL, WLAT, WLON, WPL, WLAT, WLON))  14.1 us
    another operation x3, local copies, waits for them, and re-layouts  13.2 us
    concatenate x3, local copies, waits for them, and re-layouts, block_backward(): jnp.concatenate([d_queries.reshape(lead + (window, channels)), d_keys.res...  12.4 us
    reshape x1, local copies, waits for them, and re-layouts, fold_bias(): d_bias.reshape(outer + (WPL, WLAT, WLON, WPL, WLAT, WLON))  10.1 us
    dot_general x1, matrix products, expand_bias(): jnp.einsum('pahsd,de->pahse', grouped, offset_table(), precision=lax.Prec...  7.05 us
  transfers between devices with their start and end apart: 4, of which 0 were waited for; matrix products, arithmetic and copies ran while one was open for 28% of the time, Pallas kernels for 0%

commit v1 on v0

v1 whole, which is shorter than its diff:
```python
import jax
import jax.numpy as jnp
import numpy as np
from jax import lax
from jax.experimental import pallas as pl
from jax.experimental.pallas import tpu as pltpu
from jax.sharding import PartitionSpec as P

WPL, WLAT, WLON = 2, 6, 12
WINDOW = WPL * WLAT * WLON
ROWS = WPL * WLAT
SPREAD = 2 * WLON - 1
EDGE = 16
GROUP = 4
EPSILON = 1e-05
LOG2E = 1.4426950408889634
BF = jnp.bfloat16
F32 = jnp.float32


def token_route(lon_cols):
    half_lat, half_lon = WLAT // 2, WLON // 2
    windows = lon_cols // WLON
    near = WPL * half_lat * lon_cols
    far = WPL * half_lat * EDGE
    route = np.zeros((windows * WINDOW, 2 * near + 2 * far), np.float32)
    for w in range(windows):
        for o in range(WLON):
            for l in range(WPL):
                for a in range(WLAT):
                    level = (l + 1) % WPL
                    col = w * WLON + o + half_lon
                    row = level * half_lat + a % half_lat
                    if col < lon_cols:
                        source = row * lon_cols + col + (near if a >= half_lat else 0)
                    else:
                        source = 2 * near + row * EDGE + col - lon_cols
                        source += far if a >= half_lat else 0
                    route[w * WINDOW + o * ROWS + l * WLAT + a, source] = 1.0
    return route


def head_order():
    perm = np.zeros((GROUP * WINDOW, GROUP * WINDOW), np.float32)
    for o in range(WLON):
        for h in range(GROUP):
            for r in range(ROWS):
                perm[(o * GROUP + h) * ROWS + r, (h * WLON + o) * ROWS + r] = 1.0
    return perm


def table_order():
    order = np.zeros((SPREAD * ROWS, ROWS * SPREAD), np.float32)
    for d in range(SPREAD):
        for r in range(ROWS):
            order[(SPREAD - 1 - d) * ROWS + r, r * SPREAD + d] = 1.0
    return order


def head_blocks(head_dim):
    rows = np.arange(GROUP * head_dim)[:, None] // head_dim
    cols = np.arange(GROUP * WINDOW)[None, :] // WINDOW
    return (rows == cols).astype(np.float32)


def gather_heads():
    return np.tile(np.eye(WINDOW, dtype=np.float32), (1, GROUP))


def nn(a, b):
    return lax.dot_general(a, b, (((1,), (0,)), ((), ())), preferred_element_type=F32)


def nt(a, b):
    return lax.dot_general(a, b, (((1,), (1,)), ((), ())), preferred_element_type=F32)


def tn(a, b):
    return lax.dot_general(a, b, (((0,), (0,)), ((), ())), preferred_element_type=F32)


def block_kernel(
    ids, near_x, near_c, lat_x, lat_c, lon_x, lon_c, dia_x, dia_c, route, unroute, perm, order, blocks, gather,
    table, w_qkv, w_proj, gain, shift,
    d_cat, g_weights, g_table, g_small,
    cat, normed, inv, ln, cot, qkv, d_att, att, d_qkv, bias, d_bias, folded,
):
    half_lat = WLAT // 2
    lon_cols = near_x.shape[2]
    channels = near_x.shape[3]
    near = WPL * half_lat * lon_cols
    far = WPL * half_lat * EDGE
    groups = channels // 128
    windows = lon_cols // WLON
    span = GROUP * WINDOW
    head_dim = 128 // GROUP
    scale = head_dim ** -0.5

    lane = lax.rem(lax.broadcasted_iota(jnp.int32, (1, span), 1), ROWS)
    sub = lax.rem(lax.broadcasted_iota(jnp.int32, (WINDOW, 1), 0), ROWS)
    id_q = jnp.zeros((1, span), jnp.int32)
    id_k = jnp.zeros((WINDOW, 1), jnp.int32)
    for l in range(WPL):
        for a in range(WLAT):
            value = ids[l, a]
            id_q = jnp.where(lane == l * WLAT + a, value, id_q)
            id_k = jnp.where(sub == l * WLAT + a, value, id_k)
    masked = jnp.where(id_k == id_q, 0.0, -1e30)
    folded[...] = nt(order[...], table[...])
    for g in range(groups):
        pieces = [
            folded[(WLON - 1 - o) * ROWS : (WLON - 1 - o) * ROWS + WINDOW, g * GROUP * ROWS : (g + 1) * GROUP * ROWS]
            for o in range(WLON)
        ]
        spread = jnp.concatenate(pieces, axis=1).astype(BF)
        bias[g] = nn(spread, perm[...]) * LOG2E + masked
    d_bias[...] = jnp.zeros_like(d_bias)

    for source, x, c in ((0, near_x, near_c),):
        for l in range(WPL):
            rows = pl.ds(l * half_lat * lon_cols, half_lat * lon_cols)
            cat[rows, :channels] = x[l, half_lat:].reshape(half_lat * lon_cols, channels)
            cat[rows, channels:] = c[l, half_lat:].reshape(half_lat * lon_cols, channels)
    for start, size, x, c in (
        (near, near, lat_x, lat_c), (2 * near, far, lon_x, lon_c), (2 * near + far, far, dia_x, dia_c)
    ):
        cat[start : start + size, :channels] = x[...].reshape(size, channels)
        cat[start : start + size, channels:] = c[...].reshape(size, channels)
    moved = nn(route[...], cat[...])
    x = moved[:, :channels]
    cot[...] = moved[:, channels:].astype(BF)
    average = jnp.mean(x, axis=1, keepdims=True)
    centred = x - average
    variance = jnp.mean(centred * centred, axis=1, keepdims=True)
    inv_std = lax.rsqrt(variance + EPSILON)
    inv[...] = inv_std
    norm = centred * inv_std
    normed[...] = norm
    ln[...] = (norm * gain[...] + shift[...]).astype(BF)
    qkv[...] = nn(ln[...], w_qkv[...]).astype(BF)
    d_att[...] = nt(cot[...], w_proj[...]).astype(BF)

    lanes = lax.broadcasted_iota(jnp.int32, (1, 128), 1) // head_dim
    own = [(lanes == h).astype(F32).astype(BF) for h in range(GROUP)]
    eye = (
        lax.broadcasted_iota(jnp.int32, (128, 128), 0) == lax.broadcasted_iota(jnp.int32, (128, 128), 1)
    ).astype(F32).astype(BF)

    def one_window(w, carry):
        rows = pl.ds(pl.multiple_of(w * WINDOW, WINDOW), WINDOW)
        for g in range(groups):
            cols = slice(g * 128, (g + 1) * 128)
            q = qkv[rows, g * 128 : (g + 1) * 128]
            k = qkv[rows, channels + g * 128 : channels + (g + 1) * 128]
            v = qkv[rows, 2 * channels + g * 128 : 2 * channels + (g + 1) * 128]
            da = d_att[rows, cols]
            q_heads = jnp.concatenate([q * own[h] for h in range(GROUP)], axis=0)
            da_heads = jnp.concatenate([da * own[h] for h in range(GROUP)], axis=0)
            raised = jnp.exp2(nt(k, q_heads) * (scale * LOG2E) + bias[g])
            probs = raised * (1.0 / jnp.sum(raised, axis=0, keepdims=True))
            probs_b = probs.astype(BF)
            v_t = nt(eye, v).astype(BF)
            k_t = nt(eye, k).astype(BF)
            d_probs = nt(v, da_heads)
            weighted = probs * d_probs
            d_scores = weighted - probs * jnp.sum(weighted, axis=0, keepdims=True)
            d_bias[g] += d_scores
            d_scores_b = d_scores.astype(BF)
            mask = blocks[...]
            att_t = nn(v_t, probs_b).astype(BF) * mask
            att[rows, cols] = nt(gather[...], att_t).astype(BF)
            dq_t = (nn(k_t, d_scores_b) * scale).astype(BF) * mask
            d_qkv[rows, g * 128 : (g + 1) * 128] = nt(gather[...], dq_t).astype(BF)
            d_qkv[rows, channels + g * 128 : channels + (g + 1) * 128] = (
                nn(d_scores_b, q_heads) * scale
            ).astype(BF)
            d_qkv[rows, 2 * channels + g * 128 : 2 * channels + (g + 1) * 128] = nn(probs_b, da_heads).astype(BF)
        return carry

    lax.fori_loop(0, windows, one_window, 0)

    for b in range(3):
        g_weights[b] = tn(ln[...], d_qkv[:, b * channels : (b + 1) * channels]).astype(BF)
    g_weights[3] = tn(att[...], cot[...]).astype(BF)
    d_ln = nt(d_qkv[...], w_qkv[...])
    norm = normed[...]
    g_small[...] = jnp.zeros_like(g_small)
    for g in range(groups):
        cols = slice(g * 128, (g + 1) * 128)
        g_small[g : g + 1] = jnp.sum(d_ln[:, cols] * norm[:, cols], axis=0, keepdims=True)
        g_small[groups + g : groups + g + 1] = jnp.sum(d_ln[:, cols], axis=0, keepdims=True)
    scaled = d_ln * gain[...]
    d_flat = inv[...] * (
        scaled
        - jnp.mean(scaled, axis=1, keepdims=True)
        - norm * jnp.mean(scaled * norm, axis=1, keepdims=True)
    )
    d_cat[...] = nn(unroute[...], d_flat.astype(BF)).astype(BF)

    folded[...] = jnp.zeros_like(folded)
    parts = []
    for g in range(groups):
        high = d_bias[g].astype(BF)
        low = (d_bias[g] - high.astype(F32)).astype(BF)
        parts.append(nt(high, perm[...]) + nt(low, perm[...]))
    for o in range(WLON):
        piece = jnp.concatenate([p[:, o * GROUP * ROWS : (o + 1) * GROUP * ROWS] for p in parts], axis=1)
        folded[(WLON - 1 - o) * ROWS : (WLON - 1 - o) * ROWS + WINDOW, :] += piece
    high = folded[...].astype(BF)
    low = (folded[...] - high.astype(F32)).astype(BF)
    rows = tn(high, order[...]) + tn(low, order[...])
    tail = rows[:, 256:]
    g_table[...] = jnp.concatenate(
        [
            rows[:, :128],
            rows[:, 128:256],
            jnp.concatenate([tail, jnp.zeros((tail.shape[0], 128 - tail.shape[1]), F32)], axis=1),
            jnp.zeros((PLANE * PART - 3 * rows.shape[0], 128), F32),
        ],
        axis=0,
    ).astype(BF)


def block_backward(ids, pieces, rows, w_qkv, w_proj, gain, shift):
    lon_cols, channels = pieces[0].shape[2:]
    tokens = WPL * WLAT * lon_cols
    near = WPL * (WLAT // 2) * lon_cols
    far = WPL * (WLAT // 2) * EDGE
    groups = channels // 128
    span = GROUP * WINDOW
    route = token_route(lon_cols)
    constants = [
        jnp.asarray(c, BF)
        for c in (route, route.T, head_order(), table_order(), head_blocks(128 // GROUP), gather_heads())
    ]
    vmem = pl.BlockSpec(memory_space=pltpu.VMEM)
    arrays = [*pieces, *constants, rows, w_qkv, w_proj, gain[None], shift[None]]
    return pl.pallas_call(
        block_kernel,
        out_shape=(
            jax.ShapeDtypeStruct((2 * near + 2 * far, channels), BF),
            jax.ShapeDtypeStruct((4, channels, channels), BF),
            jax.ShapeDtypeStruct((PLANE * PART, 128), BF),
            jax.ShapeDtypeStruct((8, 128), F32),
        ),
        in_specs=[pl.BlockSpec(memory_space=pltpu.SMEM)] + [vmem] * len(arrays),
        out_specs=(vmem,) * 4,
        scratch_shapes=[
            pltpu.VMEM((2 * near + 2 * far, 2 * channels), BF),
            pltpu.VMEM((tokens, channels), F32),
            pltpu.VMEM((tokens, 1), F32),
            pltpu.VMEM((tokens, channels), BF),
            pltpu.VMEM((tokens, channels), BF),
            pltpu.VMEM((tokens, 3 * channels), BF),
            pltpu.VMEM((tokens, channels), BF),
            pltpu.VMEM((tokens, channels), BF),
            pltpu.VMEM((tokens, 3 * channels), BF),
            pltpu.VMEM((groups, WINDOW, span), F32),
            pltpu.VMEM((groups, WINDOW, span), F32),
            pltpu.VMEM((SPREAD * ROWS, groups * GROUP * ROWS), F32),
        ],
        compiler_params=pltpu.CompilerParams(vmem_limit_bytes=56 * 1024 * 1024),
        cost_estimate=pl.CostEstimate(flops=6_000_000_000, bytes_accessed=10_000_000, transcendentals=1_000_000),
    )(ids, *arrays)


X_SIZE, Z_SIZE = 4, 8
PLANE = 16
USED = 7
CHUNK = 48
WEIGHT = 3 * CHUNK
PART = 32
SMALL = 16
MESH = pl.DeviceIdType.MESH


def place():
    lon = lax.axis_index("lon")
    lat = lax.axis_index("lat")
    x = lax.rem(lon, X_SIZE)
    z = lax.rem(lon // X_SIZE, Z_SIZE)
    y_lo = lon // (X_SIZE * Z_SIZE)
    y_hi = lat // 2
    core = lax.rem(lat, 2)
    return x, y_lo, y_hi, z, core


def device(plane, z, core):
    x = lax.rem(plane, X_SIZE)
    y_lo = lax.rem(plane // X_SIZE, 2)
    y_hi = plane // (2 * X_SIZE)
    return ((y_lo * Z_SIZE + z) * X_SIZE + x, y_hi * 2 + core)


def split_small(value):
    high = value.astype(BF).astype(F32)
    return jnp.concatenate([high, value - high], axis=0).astype(BF)


def reduce_kernel(
    weights, table, small,
    o_qkv, o_proj, o_table, o_small,
    small_out, core_in, small_in, plane_out, plane_in, total, z_out, z_in, z_full, full,
    core_s, core_r, small_s, small_r, plane_s, plane_r, z_s, z_r, zg_s, zg_r, pg_s, pg_r, sib_s, sib_r,
):
    x, y_lo, y_hi, z, core = place()
    me = (y_hi * 2 + y_lo) * X_SIZE + x
    sibling = device(me, z, 1 - core)
    barrier = pltpu.get_barrier_semaphore()

    def greet(target):
        pl.semaphore_signal(barrier, inc=1, device_id=target, device_id_type=MESH)

    def greet_plane(i, carry):
        greet(device(lax.rem(me + i, PLANE), z, core))
        return carry

    def greet_line(i, carry):
        greet(device(me, lax.rem(z + i, Z_SIZE), core))
        return carry

    greet(sibling)
    lax.fori_loop(1, PLANE, greet_plane, 0)
    lax.fori_loop(1, Z_SIZE, greet_line, 0)
    small_out[...] = split_small(small[...])
    pl.semaphore_wait(barrier, PLANE + Z_SIZE - 1)

    def remote(src, dst, send, recv, target):
        return pltpu.make_async_remote_copy(
            src_ref=src, dst_ref=dst, send_sem=send, recv_sem=recv, device_id=target, device_id_type=MESH
        )

    small_copy = remote(small_out, small_in, small_s.at[0], small_r.at[0], sibling)
    core_copies = [
        remote(weights.at[2 * (1 - core) + b], core_in.at[b], core_s.at[b], core_r.at[b], sibling) for b in range(2)
    ]
    for copy in core_copies:
        copy.start()
    small_copy.start()

    def plane_copy(peer):
        return remote(
            plane_out.at[peer], plane_in.at[me], plane_s.at[peer], plane_r.at[me], device(peer, z, core)
        )

    small_copy.wait()
    both = small_out[...].astype(F32) + small_in[...].astype(F32)
    small_core = split_small(both[:8] + both[8:])

    for b in range(2):
        core_copies[b].wait()

        def fill(i, carry):
            peer = b * 8 + i
            rows = pl.ds(pl.multiple_of(i * CHUNK, CHUNK), CHUNK)
            for t in range(3):
                lanes = slice(t * 128, (t + 1) * 128)
                added = weights[2 * core + b, rows, lanes].astype(F32) + core_in[b, rows, lanes].astype(F32)
                plane_out[peer, t * CHUNK : (t + 1) * CHUNK] = added.astype(BF)
            plane_out[peer, WEIGHT : WEIGHT + PART] = table[pl.ds(pl.multiple_of(peer * PART, PART), PART)]
            plane_out[peer, WEIGHT + PART :] = small_core

            @pl.when(peer != me)
            def _():
                plane_copy(peer).start()

            return carry

        lax.fori_loop(0, 8, fill, 0)

    total[...] = jnp.zeros_like(total)

    def add(part, source):
        total[:WEIGHT] += part[:WEIGHT].astype(F32)
        hi = source // (2 * X_SIZE)
        rows = pl.ds(pl.multiple_of(WEIGHT + hi * PART, PART // 2), PART)
        total[rows] += part[WEIGHT : WEIGHT + PART].astype(F32)
        total[8 * PART :] += part[WEIGHT + PART :].astype(F32)

    add(plane_out[me], me)

    def collect(i, carry):
        source = lax.rem(me + i, PLANE)
        remote(
            plane_out.at[source], plane_in.at[source], plane_s.at[source], plane_r.at[source], device(source, z, core)
        ).wait_recv()
        add(plane_in[source], source)
        return carry

    lax.fori_loop(1, PLANE, collect, 0)

    summed = total[8 * PART :]
    small_plane = split_small(summed[:8] + summed[8:])

    def z_copy(peer):
        return remote(z_out.at[peer], z_in.at[z], z_s.at[peer], z_r.at[z], device(me, peer, core))

    def fill_line(i, carry):
        peer = lax.rem(z + i, Z_SIZE)
        z_out[peer, :PART] = total[pl.ds(pl.multiple_of(peer * PART, PART), PART)].astype(BF)
        z_out[peer, PART:] = small_plane
        z_copy(peer).start()
        return carry

    lax.fori_loop(1, Z_SIZE, fill_line, 0)
    own = total[pl.ds(pl.multiple_of(z * PART, PART), PART)]
    own_small = small_plane.astype(F32)

    def collect_line(i, carry):
        part, little = carry
        source = lax.rem(z + i, Z_SIZE)
        remote(
            z_out.at[source], z_in.at[source], z_s.at[source], z_r.at[source], device(me, source, core)
        ).wait_recv()
        return part + z_in[source, :PART].astype(F32), little + z_in[source, PART:].astype(F32)

    own, own_small = lax.fori_loop(1, Z_SIZE, collect_line, (own, own_small))
    o_small[...] = own_small[:8] + own_small[8:]

    z_full[z] = own.astype(BF)

    def zg_copy(peer):
        return remote(z_full.at[z], z_full.at[z], zg_s.at[peer], zg_r.at[z], device(me, peer, core))

    def send_line(i, carry):
        zg_copy(lax.rem(z + i, Z_SIZE)).start()
        return carry

    lax.fori_loop(1, Z_SIZE, send_line, 0)

    def take_line(i, carry):
        source = lax.rem(z + i, Z_SIZE)
        remote(
            z_full.at[source], z_full.at[source], zg_s.at[source], zg_r.at[source], device(me, source, core)
        ).wait_recv()
        return carry

    lax.fori_loop(1, Z_SIZE, take_line, 0)
    full[core, me] = z_full[:USED]

    def pg_copy(peer):
        return remote(full.at[core, me], full.at[core, me], pg_s.at[peer], pg_r.at[me], device(peer, z, core))

    def sib_copy(source):
        return remote(full.at[core, source], full.at[core, source], sib_s.at[source], sib_r.at[source], sibling)

    def send_plane(i, carry):
        pg_copy(lax.rem(me + i, PLANE)).start()
        return carry

    lax.fori_loop(1, PLANE, send_plane, 0)
    sib_copy(me).start()

    def take_plane(i, carry):
        source = lax.rem(me + i, PLANE)
        remote(
            full.at[core, source], full.at[core, source], pg_s.at[source], pg_r.at[source], device(source, z, core)
        ).wait_recv()
        sib_copy(source).start()
        return carry

    lax.fori_loop(1, PLANE, take_plane, 0)

    def take_sibling(source, carry):
        remote(
            full.at[1 - core, source], full.at[1 - core, source], sib_s.at[source], sib_r.at[source], sibling
        ).wait_recv()
        return carry

    lax.fori_loop(0, PLANE, take_sibling, 0)

    def write(i, carry):
        rows = pl.ds(pl.multiple_of(i * CHUNK, CHUNK), CHUNK)
        for half in range(2):
            for b in range(2):
                block = 2 * half + b
                part = full[half, b * 8 + i].reshape(USED * PART, 128)
                for t in range(3):
                    lanes = slice((block % 3) * 384 + t * 128, (block % 3) * 384 + (t + 1) * 128)
                    target = o_qkv if block < 3 else o_proj
                    target[rows, lanes] = part[t * CHUNK : (t + 1) * CHUNK]
        return carry

    lax.fori_loop(0, 8, write, 0)

    def write_table(i, carry):
        rows = pl.ds(pl.multiple_of(i * PART, PART), PART)
        for hi in range(2):
            for half in range(2):
                part = full[half, i].reshape(USED * PART, 128)
                o_table[hi * 2 + half, rows] = part[WEIGHT + hi * PART : WEIGHT + (hi + 1) * PART]
        return carry

    lax.fori_loop(0, PLANE, write_table, 0)

    def drain_plane(i, carry):
        peer = lax.rem(me + i, PLANE)
        plane_copy(peer).wait_send()
        pg_copy(peer).wait_send()
        return carry

    def drain_line(i, carry):
        peer = lax.rem(z + i, Z_SIZE)
        z_copy(peer).wait_send()
        zg_copy(peer).wait_send()
        return carry

    def drain_sibling(source, carry):
        sib_copy(source).wait_send()
        return carry

    lax.fori_loop(1, PLANE, drain_plane, 0)
    lax.fori_loop(1, Z_SIZE, drain_line, 0)
    lax.fori_loop(0, PLANE, drain_sibling, 0)


def reduce_all(weights, table, small):
    vmem = pl.BlockSpec(memory_space=pltpu.VMEM)
    dma = pltpu.SemaphoreType.DMA
    return pl.pallas_call(
        reduce_kernel,
        out_shape=(
            jax.ShapeDtypeStruct((384, 1152), BF),
            jax.ShapeDtypeStruct((384, 384), BF),
            jax.ShapeDtypeStruct((4, PLANE * PART, 128), BF),
            jax.ShapeDtypeStruct((8, 128), F32),
        ),
        in_specs=[vmem] * 3,
        out_specs=(vmem,) * 4,
        scratch_shapes=[
            pltpu.VMEM((SMALL, 128), BF),
            pltpu.VMEM((2, 384, 384), BF),
            pltpu.VMEM((SMALL, 128), BF),
            pltpu.VMEM((PLANE, WEIGHT + PART + SMALL, 128), BF),
            pltpu.VMEM((PLANE, WEIGHT + PART + SMALL, 128), BF),
            pltpu.VMEM((Z_SIZE * PART + SMALL, 128), F32),
            pltpu.VMEM((Z_SIZE, PART + SMALL, 128), BF),
            pltpu.VMEM((Z_SIZE, PART + SMALL, 128), BF),
            pltpu.VMEM((Z_SIZE, PART, 128), BF),
            pltpu.VMEM((2, PLANE, USED, PART, 128), BF),
            dma((2,)), dma((2,)), dma((1,)), dma((1,)),
            dma((PLANE,)), dma((PLANE,)), dma((Z_SIZE,)), dma((Z_SIZE,)),
            dma((Z_SIZE,)), dma((Z_SIZE,)), dma((PLANE,)), dma((PLANE,)),
            dma((PLANE,)), dma((PLANE,)),
        ],
        compiler_params=pltpu.CompilerParams(
            collective_id=0, has_side_effects=True, vmem_limit_bytes=40 * 1024 * 1024
        ),
    )(weights, table, small)


def table_rows(table):
    heads = table.shape[0]
    split = table.reshape(heads, WPL, WPL, WLAT, WLAT * SPREAD).transpose(0, 1, 3, 2, 4)
    return split.reshape(heads * ROWS, ROWS * SPREAD)


def table_back(rows):
    heads = rows.shape[-2] // ROWS
    outer = rows.shape[:-2]
    split = rows.reshape(outer + (heads, WPL, WLAT, WPL, WLAT * SPREAD))
    split = jnp.swapaxes(split, -3, -2)
    return split.reshape(outer + (heads, -1))


def to_partner(value):
    count = lax.axis_size("lon")
    return lax.ppermute(value, "lon", [(source, source ^ 1) for source in range(count)])


def to_lat(value, steps):
    count = lax.axis_size("lat")
    return lax.ppermute(value, "lat", [(source, (source + steps) % count) for source in range(count)])


def local(tokens, cotangent, mask_ids, band_type, bias_table, w_qkv, w_proj, ln_gain, ln_shift):
    half_lon, half_lat = WLON // 2, WLAT // 2
    lon_cols = tokens.shape[2]
    channels = tokens.shape[3]
    heads = bias_table.shape[1]
    stacked = jnp.stack([tokens, cotangent])
    from_lat = to_lat(stacked[:, :, :half_lat], -1)
    from_lon = to_partner(stacked[:, :, half_lat:, :EDGE])
    from_both = to_partner(from_lat[:, :, :, :EDGE])
    lat = lax.axis_index("lat")
    own_type = lax.dynamic_index_in_dim(band_type, lat, 0, False)
    rows = table_rows(lax.dynamic_index_in_dim(bias_table, own_type, 0, False))
    pieces = [
        tokens, cotangent, from_lat[0], from_lat[1], from_lon[0], from_lon[1], from_both[0], from_both[1]
    ]
    d_cat, weights, d_rows, small = block_backward(
        mask_ids, pieces, rows, w_qkv, w_proj, ln_gain, ln_shift
    )
    near = WPL * half_lat * lon_cols
    far = WPL * half_lat * EDGE
    own = d_cat[:near].reshape(WPL, half_lat, lon_cols, channels)
    for_lat = d_cat[near : 2 * near].reshape(WPL, half_lat, lon_cols, channels)
    for_lon = d_cat[2 * near : 2 * near + far].reshape(WPL, half_lat, EDGE, channels)
    for_both = d_cat[2 * near + far :].reshape(WPL, half_lat, EDGE, channels)
    back_lon = to_partner(for_lon)
    back_both = to_partner(for_both)
    edge = jnp.arange(lon_cols)[:, None] < half_lon

    def joined(inner, outer):
        wide = jnp.pad(outer, ((0, 0), (0, 0), (0, lon_cols - EDGE), (0, 0)))
        return jnp.where(edge, wide, inner)

    top = to_lat(joined(for_lat, back_both), 1)
    low = joined(own, back_lon)
    back = jnp.concatenate([top, low], axis=1)
    grad_tokens = (cotangent.astype(F32) + back.astype(F32)).astype(BF)
    g_qkv, g_proj, tables, g_small = reduce_all(weights, d_rows, small)
    slots = band_type[None, :] == jnp.arange(band_type.shape[0])[:, None]
    ordered = jnp.take(tables, jnp.argmax(slots, axis=1), axis=0)
    ordered = ordered[:, : 3 * heads * ROWS].reshape(-1, 3, heads * ROWS, 128).swapaxes(1, 2)
    g_table = ordered.reshape(-1, heads * ROWS, 384)[:, :, : ROWS * SPREAD]
    return (
        grad_tokens,
        g_qkv,
        g_proj,
        g_small[:3].reshape(-1),
        g_small[3:6].reshape(-1),
        table_back(g_table),
    )


def solution(mesh):
    placed = (P(None, "lat", "lon", None),) * 2 + (P(None, "lat"),) + (P(),) * 6
    return jax.shard_map(
        local,
        mesh=mesh,
        in_specs=placed,
        out_specs=(P(None, "lat", "lon", None), P(), P(), P(), P(), P()),
        check_vma=False,
    )
```

time: 334 us -> 108 us (0.32); the launches traced: 328 us -> 108 us
  blocking collectives: 130 us -> 0 us
  local copies, waits for them, and re-layouts: 131 us -> 16.9 us
  Pallas kernels: 0 us -> 72.2 us
  matrix products: 36.8 us -> 0 us
  other arithmetic: 20 us -> 3.03 us
  waiting for transfers between devices: 0.01 us -> 4.18 us
    psum x1 -> x0, blocking collectives: 130 us -> none  [local(): lax.psum((g_qkv, g_proj, g_gain, g_shift, table_part), ('lon', 'lat'))]
    pallas_call x0 -> x2, Pallas kernels: none -> 72.2 us  [the longest x1 51.8 us: reduce_all(): pl.pallas_call(reduce_kernel, out_shape=(jax.ShapeDtypeStruct((384, 1152)...]
    dot_general x13 -> x0, matrix products: 36.8 us -> none  [the longest x6 15.9 us: batched(): return jnp.einsum(form, left, right, preferred_element_type=jnp.float32)]
    add x2 -> x0, local copies, waits for them, and re-layouts: 30.4 us -> none  [block_backward(): batched('pawqhd,pawkhd->pawhqk', queries, keys) * score_scale]
    transpose x5 -> x2, local copies, waits for them, and re-layouts: 23.6 us -> 0.29 us  [the longest x1 0.17 us: table_back(): split = jnp.swapaxes(split, -3, -2)]
    another operation x7 -> x0, local copies, waits for them, and re-layouts: 21.4 us -> none
    concatenate x3 -> x0, local copies, waits for them, and re-layouts: 12.4 us -> none  [block_backward(): jnp.concatenate([d_queries.reshape(lead + (window, channels)), d_keys.res...]
    mul x2 -> x0, local copies, waits for them, and re-layouts: 10.6 us -> none  [the longest x1 5.37 us: block_backward(): d_queries = batched('pawhqk,pawkhd->pawqhd', d_scores_b, keys) * score_scale]
  transfers between devices with their start and end apart: 4 -> 6, of which waited for: 0 -> 3; matrix products, arithmetic and copies ran while one was open for 28% -> 10% of each run, Pallas kernels for 0% -> 48%
where the time goes in v1:
time: 108 us
  Pallas kernels  72.2 us (67%)
  local copies, waits for them, and re-layouts  16.9 us (16%)
  starting transfers between devices  8.74 us (8%)
  waiting for transfers between devices  4.18 us (4%)
  other arithmetic  3.03 us (3%)
  between operations  2.8 us (3%)
    pallas_call x1, Pallas kernels, reduce_all(): pl.pallas_call(reduce_kernel, out_shape=(jax.ShapeDtypeStruct((384, 1152)...  51.8 us
    pallas_call x1, Pallas kernels, block_backward(): pl.pallas_call(block_kernel, out_shape=(jax.ShapeDtypeStruct((2 * near +...  20.5 us
    ppermute x2, starting transfers between devices, to_lat(): lax.ppermute(value, 'lat', [(source, (source + steps) % count) for source...  5.54 us
    unnamed x28, local copies, waits for them, and re-layouts  4.83 us
    ppermute x4, starting transfers between devices, to_partner(): lax.ppermute(value, 'lon', [(source, source ^ 1) for source in range(coun...  3.2 us
    ppermute x2, waiting for transfers between devices, to_lat(): lax.ppermute(value, 'lat', [(source, (source + steps) % count) for source...  2.36 us
  transfers between devices with their start and end apart: 6, of which 3 were waited for; matrix products, arithmetic and copies ran while one was open for 10% of the time, Pallas kernels for 48%

profile of v1, /device:TPU:1, one launch (start us, length us, event | category | flops | bytes accessed | tf_op | source)
XLA Modules:
  0.0 107.9 jit_solution(11930411742854485381)
XLA Ops:
  0.7 1.2 %fusion = bf16[2,2,3,48,384]{4,3,2,1,0:T(8,128)(2,1)S(1)} fusion(bf16[1,2,6,48,384]{4,3,2,1,0:T(8,128)(2,1)} %bitcast.37, bf16[1,2,6,48,384]{4,3,2,1,0:T(8,128)(2,1)} %bitcast.32), kind=kLoop, calls=%fused_computation.5 | loop fusion | flops 221184 | bytes 1327104 | tf_op jit(solution)/shard_map/stack | solution.py:581
  1.9 3.3 %collective-permute-start = (bf16[2,2,3,48,384]{4,3,2,1,0:T(8,128)(2,1)S(1)}, bf16[2,2,3,48,384]{4,3,2,1,0:T(8,128)(2,1)S(1)}, u32[]{:S(2)}, u32[]{:S(2)}) collective-permute-start(bf16[2,2,3,48,384]{4,3,2,1,0:T(8,128)(2,1)S(1)} %fusion), channel_id=1, source_target_pairs={{0,3},{1,0},{2,1},{3,2},{4,7},{5,4},{6,5},{7,6},{8,11},{9,8},{10,9... | collective-permute-start | bytes 1327112 | tf_op jit(solution)/shard_map/ppermute | solution.py:573
  5.4 0.6 iota_reduce_fusion
  6.0 0.6 dynamic_slice.8
  8.6 0.5 dynamic-slice_reduce_fusion
  9.0 0.4 reshape.59
  9.6 0.8 reshape.60.table
  10.4 0.6 broadcast_in_dim.35.gain
  11.0 0.6 broadcast_in_dim.36.shift
  11.5 0.7 slice_bitcast_fusion.4
  12.3 1.6 %collective-permute-start.2 = (bf16[2,2,3,16,384]{4,3,2,1,0:T(8,128)(2,1)S(1)}, bf16[2,2,3,16,384]{4,3,2,1,0:T(8,128)(2,1)S(1)}, u32[]{:S(2)}, u32[]{:S(2)}) collective-permute-start(bf16[2,2,3,16,384]{4,3,2,1,0:T(8,128)(2,1)S(1)} %slice.76), channel_id=1, source_target_pairs={{0,4},{4,0},{8,12},{12,8},{16,20},{20,16},{24,28},{28,24},{32,36},... | collective-permute-start | bytes 442376 | tf_op jit(solution)/shard_map/ppermute | solution.py:568
  13.9 0.8 slice_bitcast_fusion
  14.7 1.8 %collective-permute-done.2 = bf16[2,2,3,16,384]{4,3,2,1,0:T(8,128)(2,1)S(1)} collective-permute-done((bf16[2,2,3,16,384]{4,3,2,1,0:T(8,128)(2,1)S(1)}, bf16[2,2,3,16,384]{4,3,2,1,0:T(8,128)(2,1)S(1)}, u32[]{:S(2)}, u32[]{:S(2)}) %collective-permute-start.2) | collective-permute-done | bytes 147488 | tf_op jit(solution)/shard_map/ppermute | solution.py:568
  16.5 0.7 slice_bitcast_fusion.2
  17.2 20.5 %shard_map.190 = (bf16[768,384]{1,0:T(8,128)(2,1)}, bf16[4,384,384]{2,1,0:T(8,128)(2,1)}, bf16[512,128]{1,0:T(8,128)(2,1)}, f32[8,128]{1,0:T(8,128)}) custom-call(s32[2,6]{1,0:T(2,128)} %ids.1, bf16[2,6,48,384]{3,2,1,0:T(8,128)(2,1)} %near_x.1, bf16[2,6,48,384]{3,2,1,0:T(8,128)(2,1)} %near_c.1, bf16[2,3,48,384]{3,2,1,0:T(8,128)(2,1)} %get-tuple-element.29.lat_x, ...), custom_call_target="tpu_custom_call" | custom-call | flops 6000000000 | bytes 10000000 | tf_op jit(solution)/shard_map/pallas_call | solution.py:238
  37.7 1.6 %fusion.1 = (bf16[96,384]{1,0:T(8,128)(2,1)}, bf16[96,384]{1,0:T(8,128)(2,1)}) fusion(bf16[768,384]{1,0:T(8,128)(2,1)} %get-tuple-element.15), kind=kLoop, calls=%fused_computation.25 | loop fusion | bytes 294912 | tf_op jit(solution)/shard_map/slice | solution.py:599
  39.3 1.4 %collective-permute-start.3 = (bf16[2,3,16,384]{3,2,1,0:T(8,128)(2,1)}, bf16[2,3,16,384]{3,2,1,0:T(8,128)(2,1)S(1)}, u32[]{:S(2)}, u32[]{:S(2)}) collective-permute-start(bf16[2,3,16,384]{3,2,1,0:T(8,128)(2,1)} %bitcast.10), channel_id=1, source_target_pairs={{0,4},{4,0},{8,12},{12,8},{16,20},{20,16},{24,28},{28,24},{32,36},... | collective-permute-start | bytes 221192 | tf_op jit(solution)/shard_map/ppermute | solution.py:568
  40.8 1.3 %copy-done.1 = bf16[4,384,384]{2,1,0:T(8,128)(2,1)S(1)} copy-done((bf16[4,384,384]{2,1,0:T(8,128)(2,1)S(1)}, bf16[4,384,384]{2,1,0:T(8,128)(2,1)}, u32[]{:S(2)}) %copy-start.1) | copy-done | bytes 1179672
  42.0 0.9 copy-done.2
  42.9 0.7 copy-done.3
  43.6 51.8 %shard_map.191 = (bf16[384,1152]{1,0:T(8,128)(2,1)S(1)}, bf16[384,384]{1,0:T(8,128)(2,1)S(1)}, bf16[4,512,128]{2,1,0:T(8,128)(2,1)S(1)}, f32[8,128]{1,0:T(8,128)S(1)}) custom-call(bf16[4,384,384]{2,1,0:T(8,128)(2,1)S(1)} %copy-done.1, bf16[512,128]{1,0:T(8,128)(2,1)S(1)} %copy-done.2, f32[8,128]{1,0:T(8,128)S(1)} %copy-done.3), custom_call_target="tpu_custom_call" | custom-call | tf_op jit(solution)/shard_map/pallas_call | solution.py:520
  95.4 0.6 gather_fusion
  96.2 0.3 copy-done.9
  96.4 0.8 fusion.2
  97.5 0.4 reshape.68
  98.3 1.8 %reshape.70 = bf16[4,12,3312]{2,0,1:T(4,128)(2,1)} reshape(bf16[4,12,2,2,6,138]{5,4,3,2,0,1:T(8,128)(2,1)S(1)} %copy.26) | data formatting | bytes 635904 | tf_op jit(solution)/shard_map/reshape | solution.py:563
  100.3 2.2 %collective-permute-start.4 = (bf16[2,3,48,384]{3,2,1,0:T(8,128)(2,1)S(1)}, bf16[2,3,48,384]{3,2,1,0:T(8,128)(2,1)S(1)}, u32[]{:S(2)}, u32[]{:S(2)}) collective-permute-start(bf16[2,3,48,384]{3,2,1,0:T(8,128)(2,1)S(1)} %get-tuple-element.36), channel_id=1, source_target_pairs={{0,1},{1,2},{2,3},{3,0},{4,5},{5,6},{6,7},{7,4},{8,9},{9,10},{10,1... | collective-permute-start | bytes 663560 | tf_op jit(solution)/shard_map/ppermute | solution.py:573
  102.5 0.6 slice_bitcast_fusion.6
  103.1 2.3 %collective-permute-done.4 = bf16[2,3,48,384]{3,2,1,0:T(8,128)(2,1)S(1)} collective-permute-done((bf16[2,3,48,384]{3,2,1,0:T(8,128)(2,1)S(1)}, bf16[2,3,48,384]{3,2,1,0:T(8,128)(2,1)S(1)}, u32[]{:S(2)}, u32[]{:S(2)}) %collective-permute-start.4) | collective-permute-done | bytes 221216 | tf_op jit(solution)/shard_map/ppermute | solution.py:573
  105.4 0.9 add_convert_fusion
  106.3 0.9 copy.31
  107.2 0.7 copy.32
  (40 shorter events, 1.4 us)
Async XLA Ops:
  0.6 7.9 %copy-start = (bf16[4,12,3312]{2,0,1:T(4,128)(2,1)S(1)}, bf16[4,12,3312]{2,0,1:T(4,128)(2,1)}, u32[]{:S(2)}) copy-start(bf16[4,12,3312]{2,0,1:T(4,128)(2,1)} %param.19) | copy-start | bytes 953860
  0.6 4.6 %copy-start.6 = (bf16[2,6,48,384]{3,2,1,0:T(8,128)(2,1)S(1)}, bf16[2,6,48,384]{3,2,1,0:T(8,128)(2,1)}, u32[]{:S(2)}) copy-start(bf16[2,6,48,384]{3,2,1,0:T(8,128)(2,1)} %near_x.1) | copy-start | bytes 1327108
  0.7 4.6 %copy-start.4 = (bf16[2,6,48,384]{3,2,1,0:T(8,128)(2,1)S(1)}, bf16[2,6,48,384]{3,2,1,0:T(8,128)(2,1)}, u32[]{:S(2)}) copy-start(bf16[2,6,48,384]{3,2,1,0:T(8,128)(2,1)} %near_c.1) | copy-start | bytes 1327108
  0.7 4.7 %copy-start.12 = (s32[4]{0:T(128)S(1)}, s32[4]{0:T(128)}, u32[]{:S(2)}) copy-start(s32[4]{0:T(128)} %param.18) | copy-start | bytes 52
  1.9 8.5 %copy-start.10 = (f32[384]{0:T(512)S(1)}, f32[384]{0:T(512)}, u32[]{:S(2)}) copy-start(f32[384]{0:T(512)} %param.22) | copy-start | bytes 4612
  1.9 9.1 %copy-start.11 = (f32[384]{0:T(512)S(1)}, f32[384]{0:T(512)}, u32[]{:S(2)}) copy-start(f32[384]{0:T(512)} %param.23) | copy-start | bytes 4612
  1.9 10.4 %collective-permute-start = (bf16[2,2,3,48,384]{4,3,2,1,0:T(8,128)(2,1)S(1)}, bf16[2,2,3,48,384]{4,3,2,1,0:T(8,128)(2,1)S(1)}, u32[]{:S(2)}, u32[]{:S(2)}) collective-permute-start(bf16[2,2,3,48,384]{4,3,2,1,0:T(8,128)(2,1)S(1)} %fusion), channel_id=1, source_target_pairs={{0,3},{1,0},{2,1},{3,2},{4,7},{5,4},{6,5},{7,6},{8,11},{9,8},{10,9... | collective-permute-start | bytes 1327112 | tf_op jit(solution)/shard_map/ppermute | solution.py:573
  5.2 6.3 %collective-permute-start.1 = (bf16[2,2,3,16,384]{4,3,2,1,0:T(8,128)(2,1)S(1)}, bf16[2,2,3,16,384]{4,3,2,1,0:T(8,128)(2,1)S(1)}, u32[]{:S(2)}, u32[]{:S(2)}) collective-permute-start(bf16[2,2,3,16,384]{4,3,2,1,0:T(8,128)(2,1)S(1)} %pad_maximum_fusion), channel_id=1, source_target_pairs={{0,4},{4,0},{8,12},{12,8},{16,20},{20,16},{24,28},{28,24},{32,36},... | collective-permute-start | bytes 442376 | tf_op jit(solution)/shard_map/ppermute | solution.py:568
  12.3 4.3 %collective-permute-start.2 = (bf16[2,2,3,16,384]{4,3,2,1,0:T(8,128)(2,1)S(1)}, bf16[2,2,3,16,384]{4,3,2,1,0:T(8,128)(2,1)S(1)}, u32[]{:S(2)}, u32[]{:S(2)}) collective-permute-start(bf16[2,2,3,16,384]{4,3,2,1,0:T(8,128)(2,1)S(1)} %slice.76), channel_id=1, source_target_pairs={{0,4},{4,0},{8,12},{12,8},{16,20},{20,16},{24,28},{28,24},{32,36},... | collective-permute-start | bytes 442376 | tf_op jit(solution)/shard_map/ppermute | solution.py:568
  39.3 60.8 %collective-permute-start.3 = (bf16[2,3,16,384]{3,2,1,0:T(8,128)(2,1)}, bf16[2,3,16,384]{3,2,1,0:T(8,128)(2,1)S(1)}, u32[]{:S(2)}, u32[]{:S(2)}) collective-permute-start(bf16[2,3,16,384]{3,2,1,0:T(8,128)(2,1)} %bitcast.10), channel_id=1, source_target_pairs={{0,4},{4,0},{8,12},{12,8},{16,20},{20,16},{24,28},{28,24},{32,36},... | collective-permute-start | bytes 221192 | tf_op jit(solution)/shard_map/ppermute | solution.py:568
  40.7 59.4 %collective-permute-start.5 = (bf16[2,3,16,384]{3,2,1,0:T(8,128)(2,1)}, bf16[2,3,16,384]{3,2,1,0:T(8,128)(2,1)S(1)}, u32[]{:S(2)}, u32[]{:S(2)}) collective-permute-start(bf16[2,3,16,384]{3,2,1,0:T(8,128)(2,1)} %bitcast.12), channel_id=1, source_target_pairs={{0,4},{4,0},{8,12},{12,8},{16,20},{20,16},{24,28},{28,24},{32,36},... | collective-permute-start | bytes 221192 | tf_op jit(solution)/shard_map/ppermute | solution.py:568
  40.8 1.3 %copy-start.1 = (bf16[4,384,384]{2,1,0:T(8,128)(2,1)S(1)}, bf16[4,384,384]{2,1,0:T(8,128)(2,1)}, u32[]{:S(2)}) copy-start(bf16[4,384,384]{2,1,0:T(8,128)(2,1)} %get-tuple-element.16.weights) | copy-start | bytes 3538948
  42.0 0.9 copy-start.2
  42.9 0.7 copy-start.3
  95.4 1.1 copy-start.9
  98.3 1.8 %copy-start.7 = (bf16[288,384]{1,0:T(8,128)(2,1)S(1)}, bf16[288,384]{1,0:T(8,128)(2,1)}, u32[]{:S(2)}) copy-start(bf16[288,384]{1,0:T(8,128)(2,1)} %get-tuple-element.26) | copy-start | bytes 663556
  98.3 1.8 %copy-start.8 = (bf16[288,384]{1,0:T(8,128)(2,1)S(1)}, bf16[288,384]{1,0:T(8,128)(2,1)}, u32[]{:S(2)}) copy-start(bf16[288,384]{1,0:T(8,128)(2,1)} %get-tuple-element.27) | copy-start | bytes 663556
  98.3 7.1 %copy-start.5 = (bf16[2,6,48,384]{3,2,1,0:T(8,128)(2,1)S(1)}, bf16[2,6,48,384]{3,2,1,0:T(8,128)(2,1)}, u32[]{:S(2)}) copy-start(bf16[2,6,48,384]{3,2,1,0:T(8,128)(2,1)} %near_c.1) | copy-start | bytes 1327108
  100.3 5.1 %collective-permute-start.4 = (bf16[2,3,48,384]{3,2,1,0:T(8,128)(2,1)S(1)}, bf16[2,3,48,384]{3,2,1,0:T(8,128)(2,1)S(1)}, u32[]{:S(2)}, u32[]{:S(2)}) collective-permute-start(bf16[2,3,48,384]{3,2,1,0:T(8,128)(2,1)S(1)} %get-tuple-element.36), channel_id=1, source_target_pairs={{0,1},{1,2},{2,3},{3,0},{4,5},{5,6},{6,7},{7,4},{8,9},{9,10},{10,1... | collective-permute-start | bytes 663560 | tf_op jit(solution)/shard_map/ppermute | solution.py:573
